TPU v7x, 256 devices: a whole 4x4x8 slice. The times are simulated.
256 devices in a mesh: group: 4 (over x), shard: 64 (over z, y, core).
Axes of the slice: x: 4, y: 4, z: 8, core: 2. Of those that a mesh axis runs over, the one named last changes fastest.
Arguments:
- delta: float32 [4, 3072, 5120], P('group', 'shard'), as said below
- error: float32 [4, 3072, 5120], P('group', 'shard'), may hold values from -4 to 4
- weights: float32 [3072, 5120], P('shard'), may hold values from -0.75 to 0.75
- momentum: float32 [3072, 5120], P('shard'), may hold values from -3 to 3
- anchor: float32 [3072, 5120], P('shard'), may hold values from -0.75 to 0.75
- basis: float32 [5120, 64], replicated, may hold values from -0.078125 to 0.078125
Outputs:
- new_weights: float32 [3072, 5120], P('shard')
- new_momentum: float32 [3072, 5120], P('shard')
- new_anchor: float32 [3072, 5120], P('shard')
- new_error: float32 [4, 3072, 5120], P('group', 'shard')
- new_basis: float32 [5120, 64], replicated
Inputs may be any that keep to these rules, and one draw needn't show every extreme that they name: `delta`: Real-valued pseudo-gradients of full rank.
All inputs are finite; a program needn't handle non-finite values.
Results may differ from a plain program's by a relative error of at most 0.00027.
Values sent between devices are 32-bit elements; how exact they have to be, the bound alone decides.
A program may use at most 64 MiB of HBM per device.

v0:
```python
import jax
import jax.numpy as jnp
from jax import lax
from jax.sharding import PartitionSpec as P

outer_rate = 0.7
nesterov_mu = 0.9
anchor_decay = 0.9


def per_device(delta, error, weights, momentum, anchor, basis):
    highest = lax.Precision.HIGHEST
    merged = (delta + error)[0]
    local_left = jnp.dot(merged, basis, precision=highest, preferred_element_type=jnp.float32)
    left = lax.psum(local_left, "group")
    local_gram = jnp.dot(left.T, left, precision=highest, preferred_element_type=jnp.float32)
    gram = lax.psum(local_gram, "shard")
    chol = jnp.linalg.cholesky(gram)
    ortho = jax.scipy.linalg.solve_triangular(chol, left.T, lower=True).T
    groups = lax.axis_size("group")
    term = jnp.dot(merged.T, ortho, precision=highest, preferred_element_type=jnp.float32)
    right = lax.psum(term, ("group", "shard"))
    new_basis = right / groups
    approx = jnp.dot(ortho, new_basis.T, precision=highest, preferred_element_type=jnp.float32)
    new_error = (merged - approx)[None]
    new_momentum = nesterov_mu * momentum + approx
    new_weights = weights - outer_rate * (approx + nesterov_mu * new_momentum)
    new_anchor = anchor_decay * anchor + (1.0 - anchor_decay) * new_weights
    return (new_weights, new_momentum, new_anchor, new_error, new_basis)


def solution(mesh):
    in_specs = (
        P("group", "shard", None),
        P("group", "shard", None),
        P("shard", None),
        P("shard", None),
        P("shard", None),
        P(),
    )
    out_specs = (
        P("shard", None),
        P("shard", None),
        P("shard", None),
        P("group", "shard", None),
        P(),
    )
    return jax.shard_map(
        per_device, mesh=mesh, in_specs=in_specs, out_specs=out_specs, check_vma=False
    )
```

profile of v0, /device:TPU:1, one launch (start us, length us, event | category | flops | bytes accessed | tf_op | source)
XLA Modules:
  0.0 559.9 jit_solution(10521740840862063540)
XLA Ops:
  7.2 0.0 copy-start
  7.2 0.0 copy-start.2
  7.2 0.0 copy-start.1
  7.2 0.0 all-reduce.2.cloned.1.call-start
  7.2 1.2 copy-done
  8.5 2.7 fusion.2
  11.2 14.4 %psum.21 = f32[48,64]{1,0:T(8,128)S(1)} all-reduce(f32[48,64]{1,0:T(8,128)S(1)} %fusion.2), channel_id=1, replica_groups=mesh['group'=4,'shard'=64] {'group'}, use_global_device_ids=true, to_apply=%region_0.0 | all-reduce | flops 3072 | bytes 24576 | tf_op jit(solution)/shard_map/psum | solution.py:15
  25.5 0.2 fusion.11
  25.8 248.6 %psum.22 = f32[64,64]{0,1:T(8,128)S(1)} all-reduce(f32[64,64]{0,1:T(8,128)S(1)} %fusion.11), channel_id=1, replica_groups=mesh['group'=4,'shard'=64] {'shard'}, use_global_device_ids=true, to_apply=%region_1.0 | all-reduce | flops 4096 | bytes 32768 | tf_op jit(solution)/shard_map/psum | solution.py:17
  274.4 0.1 copy.12
  274.5 5.8 %cholesky.16 = f32[64,64]{1,0:T(8,128)S(1)} custom-call(f32[64,64]{1,0:T(8,128)S(1)} %fusion.8), custom_call_target="Cholesky" | custom-call | tf_op jit(solution)/shard_map/jit(cholesky)/cholesky | solution.py:18
  280.4 0.6 compare_reduce_fusion
  281.0 0.7 fusion.5
  281.7 4.9 custom-call.7
  286.6 0.2 fusion.6
  286.7 0.0 copy-done.2
  286.8 0.0 copy-done.1
  286.8 2.3 fusion
  289.1 0.0 all-reduce.2.cloned.1.call-update
  289.1 257.1 %all-reduce.2.cloned.1.call-done = f32[5120,64]{0,1:T(8,128)} async-done(((f32[5120,64]{0,1:T(8,128)}), f32[5120,64]{0,1:T(8,128)}) %all-reduce.2.cloned.1.call-update) | async-done | bytes 1310736 | tf_op jit(solution)/shard_map/psum | solution.py:22
  546.2 0.0 copy-start.4
  546.2 0.0 copy-start.5
  546.2 1.6 broadcast_multiply_fusion
  547.8 0.0 copy-done.4
  547.8 0.3 copy-done.5
  548.1 0.0 copy-start.3
  548.1 5.0 multiply_add_fusion
  553.1 0.0 copy-done.3
  (2 shorter events, 0.0 us)
Async XLA Ops:
  7.2 1.3 copy-start
  7.2 279.6 %copy-start.2 = (f32[1,48,5120]{2,1,0:T(8,128)S(1)}, f32[1,48,5120]{2,1,0:T(8,128)}, u32[]{:S(2)}) copy-start(f32[1,48,5120]{2,1,0:T(8,128)} %param.7) | copy-start | bytes 2949124
  7.2 279.6 %copy-start.1 = (f32[1,48,5120]{2,1,0:T(8,128)S(1)}, f32[1,48,5120]{2,1,0:T(8,128)}, u32[]{:S(2)}) copy-start(f32[1,48,5120]{2,1,0:T(8,128)} %param.6) | copy-start | bytes 2949124
  7.2 539.0 %all-reduce.2.cloned.1.call-start = ((), (), s32[]{:S(2)}) async-start(), calls=%async_computation | async-start | bytes 2621440 | tf_op jit(solution)/shard_map/psum | solution.py:22
  546.2 1.6 copy-start.4
  546.2 1.9 copy-start.5
  548.1 5.0 copy-start.3
Sparse Core Ops, SparseCore 0:
  289.2 256.9 all-reduce.1
where the time goes:
time: 561 us; the launch traced here: 560 us
  blocking collectives  263 us (47%)
  waiting for transfers between devices  257 us (46%)
  between operations  14.1 us (3%)
  other arithmetic  13.6 us (2%)
  matrix products  10.3 us (2%)
    psum x1, waiting for transfers between devices, per_device(): right = lax.psum(term, ('group', 'shard'))  257 us
    psum x1, blocking collectives, per_device(): gram = lax.psum(local_gram, 'shard')  249 us
    psum x1, blocking collectives, per_device(): left = lax.psum(local_left, 'group')  14.4 us
  transfers between devices with their start and end apart: 1, of which 1 were waited for; matrix products, arithmetic and copies ran while one was open for 0% of the time, Pallas kernels for 0%

commit v1 on v0

v1 whole, which is shorter than its diff:
```python
import jax
import jax.numpy as jnp
from jax import lax
from jax.experimental import pallas as pl
from jax.experimental.pallas import tpu as pltpu
from jax.sharding import PartitionSpec as P

MESH = pl.DeviceIdType.MESH
HIGHEST = lax.Precision.HIGHEST
F32 = jnp.float32

outer_rate = 0.7
nesterov_mu = 0.9
anchor_decay = 0.9

D = 5120
RANK = 64
ROWS = 48
NX, NY, NZ = 4, 4, 8
HALF = D // 2
QUARTER = HALF // 4
CHUNKS = ((0, 384), (384, 256))
LOAD = 1280
ZORDER = (4, 3, 5, 2, 6, 1, 7)


def hint(value, multiple):
    return pl.multiple_of(value, multiple)


def dot_nt(a, b):
    return lax.dot_general(a, b, (((1,), (1,)), ((), ())), precision=HIGHEST, preferred_element_type=F32)


def dot_tn(a, b):
    return lax.dot_general(a, b, (((0,), (0,)), ((), ())), precision=HIGHEST, preferred_element_type=F32)


def dot(a, b):
    return jnp.dot(a, b, precision=HIGHEST, preferred_element_type=F32)


def eliminate(aug, first, last):
    for j in range(first, last):
        block = j // 8 * 8
        pivot = aug[j : j + 1, j : j + 1]
        scale = lax.rsqrt(pivot)
        scale = scale * (1.5 - 0.5 * pivot * scale * scale)
        row = aug[j : j + 1, :] * scale
        tail = aug[block:, :]
        index = lax.broadcasted_iota(jnp.int32, tail.shape, 0) + block
        moved = tail - (tail[:, j : j + 1] * scale) * row
        tail = jnp.where(index > j, moved, jnp.where(index == j, row, tail))
        aug[block:, :] = tail


def reduce_kernel(
    delta, error, basis_t, merged, total, coef,
    d_buf, e_buf, b_buf, mcat, lbuf, l96, tsend, p1, s1, p2, p3, gfull, gy, gz, gsum, aug,
    load_sem, sib_sem, left_sem, p1_sem, p2_sem, p3_sem, p4_sem, p5_sem, fwd_sem, gy_sem, gz_sem, gs_sem,
):
    x = lax.axis_index("group")
    shard = lax.axis_index("shard")
    z = shard // 8
    y = (shard // 2) % 4
    c = shard % 2

    def device(dx, dy, dz, dc):
        return ((x + dx) % NX, ((z + dz) % NZ) * 8 + ((y + dy) % NY) * 2 + (c + dc) % 2)

    def first_axis(d):
        return device(d * (1 - c), d * c, 0, 0)

    def last_axis(d):
        return device(d * c, d * (1 - c), 0, 0)

    sibling = device(0, 0, 0, 1)
    quarter = x * (1 - c) + y * c
    other = y * (1 - c) + x * c

    barrier = pltpu.get_barrier_semaphore()
    peers = [device(dx, 0, 0, dc) for dc in range(2) for dx in range(NX) if dx or dc]
    peers += [device(0, d, 0, 0) for d in range(1, NY)]
    peers += [device(0, 0, d, 0) for d in range(1, NZ)]
    for peer in peers:
        pl.semaphore_signal(barrier, inc=1, device_id=peer, device_id_type=MESH)

    columns = [hint(((1 - c) * HALF + k * LOAD) % D, 128) for k in range(D // LOAD)]
    loads = []
    for k, col in enumerate(columns):
        cols = pl.ds(col, LOAD)
        group = []
        for j, (src, dst) in enumerate(((delta, d_buf), (error, e_buf), (basis_t, b_buf))):
            copy = pltpu.make_async_copy(src.at[:, cols], dst.at[:, cols], load_sem.at[k, j])
            copy.start()
            group.append(copy)
        loads.append(group)

    pending = []

    def send(src, dst, sems, index, peer):
        copy = pltpu.make_async_remote_copy(
            src_ref=src, dst_ref=dst, send_sem=sems.at[(0, *index)], recv_sem=sems.at[(1, *index)],
            device_id=peer, device_id_type=MESH,
        )
        copy.start()
        pending.append(copy)
        return copy

    mine = pl.ds(hint(c * ROWS, 8), ROWS)
    part = jnp.zeros((ROWS, RANK), F32)
    moved = None
    for k, col in enumerate(columns):
        for copy in loads[k]:
            copy.wait()
        cols = pl.ds(col, LOAD)
        value = d_buf[:, cols] + e_buf[:, cols]
        merged[:, cols] = value
        if k >= 2:
            mcat[mine, (k - 2) * LOAD : (k - 1) * LOAD] = value
        part = part + dot_nt(value, b_buf[:, cols])
        if k == 1:
            pl.semaphore_wait(barrier, len(peers))
            theirs = pl.ds(hint((1 - c) * HALF, 128), HALF)
            moved = send(merged.at[:, theirs], mcat.at[mine, :], sib_sem, (0,), sibling)

    lbuf[c, x] = jnp.zeros((ROWS, 2 * RANK), F32)
    lbuf[c, x, :, 0:RANK] = part
    lefts = []
    for dx, dc in ((2, 0), (2, 1), (1, 0), (3, 0), (1, 1), (3, 1), (0, 1)):
        lefts.append(send(lbuf.at[c, x], lbuf.at[c, x], left_sem, (dc * 4 + dx,), device(dx, 0, 0, dc)))
    for copy in lefts:
        copy.wait_recv()
    for core in range(2):
        l96[core * ROWS : (core + 1) * ROWS, :] = (
            (lbuf[core, 0] + lbuf[core, 1]) + lbuf[core, 2]
        ) + lbuf[core, 3]
    left = l96[...]
    left_t = jnp.transpose(left)[:RANK, :]
    moved.wait_recv()

    first = []
    for n, (off, width) in enumerate(CHUNKS):
        copies = []
        for d in (2, 1, 3, 0):
            start = hint(((quarter + d) % 4) * QUARTER + off, 128)
            tsend[d, :, off : off + width] = dot(left_t, mcat[:, pl.ds(start, width)])
            if d:
                piece = (d, slice(None), pl.ds(off, width))
                copies.append(send(tsend.at[piece], p1.at[piece], p1_sem, (n, d), first_axis(d)))
        first.append(copies)

    gfull[...] = dot(left_t, left)
    half = pl.ds(hint(c * 32, 32), 32)
    gy[y] = gfull[half, :]
    copies = [send(gy.at[y], gy.at[y], gy_sem, (d,), device(0, d, 0, 0)) for d in (2, 1, 3)]
    for copy in copies:
        copy.wait_recv()
    gz[z] = ((gy[0] + gy[1]) + gy[2]) + gy[3]
    gram_z = [send(gz.at[z], gz.at[z], gz_sem, (d,), device(0, 0, d, 0)) for d in ZORDER]

    second = [None] * len(CHUNKS)
    third = [None] * len(CHUNKS)
    fourth = [None] * len(CHUNKS)
    fifth = [None] * len(CHUNKS)
    base = c * HALF + quarter * QUARTER
    rows = pl.ds(hint(z * 8, 8), 8)

    def stage1(n):
        off, width = CHUNKS[n]
        cols = pl.ds(off, width)
        for copy in first[n]:
            copy.wait_recv()
        s1[:, cols] = ((tsend[0, :, cols] + p1[1, :, cols]) + p1[2, :, cols]) + p1[3, :, cols]
        second[n] = []
        for d in ZORDER:
            out = pl.ds(hint(((z + d) % NZ) * 8, 8), 8)
            second[n].append(send(s1.at[out, cols], p2.at[d, :, cols], p2_sem, (n, d), device(0, 0, d, 0)))

    def stage2(n):
        off, width = CHUNKS[n]
        cols = pl.ds(off, width)
        for copy in second[n]:
            copy.wait_recv()
        value = s1[rows, cols]
        for d in range(1, NZ):
            value = value + p2[d, :, cols]
        p3[other, :, cols] = value
        piece = (other, slice(None), cols)
        third[n] = [send(p3.at[piece], p3.at[piece], p3_sem, (n, d), last_axis(d)) for d in (2, 1, 3)]

    def stage3(n):
        off, width = CHUNKS[n]
        cols = pl.ds(off, width)
        for copy in third[n]:
            copy.wait_recv()
        place = (rows, pl.ds(hint(base + off, 128), width))
        total[place] = ((p3[0, :, cols] + p3[1, :, cols]) + p3[2, :, cols]) + p3[3, :, cols]
        fourth[n] = [send(total.at[place], total.at[place], p4_sem, (n, d), device(0, 0, d, 0)) for d in ZORDER]

    def stage4(n):
        off, width = CHUNKS[n]
        for copy in fourth[n]:
            copy.wait_recv()
        place = (slice(None), pl.ds(hint(base + off, 128), width))
        fifth[n] = [send(total.at[place], total.at[place], p5_sem, (n, d), first_axis(d)) for d in (2, 1, 3)]
        fifth[n].append(send(total.at[place], total.at[place], fwd_sem, (n, 0), sibling))

    def stage5(n):
        off, width = CHUNKS[n]
        for i, d in ((1, 1), (2, 3), (0, 2)):
            fifth[n][i].wait_recv()
            start = hint(c * HALF + ((quarter + 4 - d) % 4) * QUARTER + off, 128)
            place = (slice(None), pl.ds(start, width))
            fifth[n].append(send(total.at[place], total.at[place], fwd_sem, (n, d), sibling))

    def stage6(n):
        for copy in fifth[n][3:]:
            copy.wait_recv()

    def gram_stage():
        for copy in gram_z:
            copy.wait_recv()
        value = gz[0]
        for k in range(1, NZ):
            value = value + gz[k]
        gsum[half, :] = value
        swap = send(gsum.at[half], gsum.at[half], gs_sem, (0,), sibling)
        swap.wait_recv()
        lane = lax.broadcasted_iota(jnp.int32, (RANK, 2 * RANK), 1)
        row = lax.broadcasted_iota(jnp.int32, (RANK, 2 * RANK), 0)
        aug[...] = jnp.where(lane < RANK, gsum[...], jnp.where(lane - RANK == row, 1.0, 0.0))

    def coefficients():
        inverse = pltpu.roll(aug[...], RANK, 1)[:, :RANK]
        own = l96[mine, 0:RANK]
        ortho = dot_nt(own, inverse)
        coef[0:RANK, :] = 0.25 * inverse
        coef[RANK : RANK + ROWS, :] = 0.25 * dot(ortho, inverse)

    count = len(CHUNKS)
    stages = (stage1, stage2, stage3, stage4, stage5, stage6)
    for step in range(len(stages) + count - 1):
        for n in range(count):
            if 0 <= step - n < len(stages):
                stages[step - n](n)
        if step == 0:
            gram_stage()
        elif step == 1:
            eliminate(aug, 0, 32)
        elif step == 2:
            eliminate(aug, 32, RANK)
        elif step == 3:
            coefficients()

    for copy in pending:
        copy.wait_send()


def update_kernel(merged, total, coef, weights, momentum, anchor, new_weights, new_momentum, new_anchor, new_error, new_basis):
    both = dot(coef[...], total[...])
    new_basis[...] = both[:RANK]
    approx = both[RANK:]
    new_error[...] = merged[...] - approx
    moved = nesterov_mu * momentum[...] + approx
    new_momentum[...] = moved
    stepped = weights[...] - outer_rate * (approx + nesterov_mu * moved)
    new_weights[...] = stepped
    new_anchor[...] = anchor_decay * anchor[...] + (1.0 - anchor_decay) * stepped


def per_device(delta, error, weights, momentum, anchor, basis):
    count = len(CHUNKS)
    hbm = pl.BlockSpec(memory_space=pl.ANY)
    vmem = pl.BlockSpec(memory_space=pltpu.VMEM)
    dma = pltpu.SemaphoreType.DMA
    merged, total, coef = pl.pallas_call(
        reduce_kernel,
        out_shape=(
            jax.ShapeDtypeStruct((ROWS, D), F32),
            jax.ShapeDtypeStruct((RANK, D), F32),
            jax.ShapeDtypeStruct((RANK + ROWS, RANK), F32),
        ),
        in_specs=[hbm, hbm, hbm],
        out_specs=(vmem, vmem, vmem),
        scratch_shapes=[
            pltpu.VMEM((ROWS, D), F32),
            pltpu.VMEM((ROWS, D), F32),
            pltpu.VMEM((RANK, D), F32),
            pltpu.VMEM((2 * ROWS, HALF), F32),
            pltpu.VMEM((2, NX, ROWS, 2 * RANK), F32),
            pltpu.VMEM((2 * ROWS, 2 * RANK), F32),
            pltpu.VMEM((4, RANK, QUARTER), F32),
            pltpu.VMEM((4, RANK, QUARTER), F32),
            pltpu.VMEM((RANK, QUARTER), F32),
            pltpu.VMEM((NZ, 8, QUARTER), F32),
            pltpu.VMEM((4, 8, QUARTER), F32),
            pltpu.VMEM((RANK, 2 * RANK), F32),
            pltpu.VMEM((NY, 32, 2 * RANK), F32),
            pltpu.VMEM((NZ, 32, 2 * RANK), F32),
            pltpu.VMEM((RANK, 2 * RANK), F32),
            pltpu.VMEM((RANK, 2 * RANK), F32),
            dma((D // LOAD, 3)),
            dma((2, 1)),
            dma((2, 8)),
            dma((2, count, 4)),
            dma((2, count, 8)),
            dma((2, count, 4)),
            dma((2, count, 8)),
            dma((2, count, 4)),
            dma((2, count, 4)),
            dma((2, 4)),
            dma((2, 8)),
            dma((2, 1)),
        ],
        compiler_params=pltpu.CompilerParams(collective_id=0, has_side_effects=True, vmem_limit_bytes=32 << 20),
    )(delta[0], error[0], basis.T)

    block = 1024

    def cols(height):
        return pl.BlockSpec((height, block), lambda i: (0, i))

    outs = pl.pallas_call(
        update_kernel,
        grid=(D // block,),
        out_shape=[jax.ShapeDtypeStruct((ROWS, D), F32)] * 4 + [jax.ShapeDtypeStruct((RANK, D), F32)],
        in_specs=[cols(ROWS), cols(RANK), pl.BlockSpec((RANK + ROWS, RANK), lambda i: (0, 0)), cols(ROWS), cols(ROWS), cols(ROWS)],
        out_specs=[cols(ROWS)] * 4 + [cols(RANK)],
    )(merged, total, coef, weights, momentum, anchor)
    new_weights, new_momentum, new_anchor, new_error, new_basis = outs
    return (new_weights, new_momentum, new_anchor, new_error[None], new_basis.T)


def solution(mesh):
    in_specs = (
        P("group", "shard", None),
        P("group", "shard", None),
        P("shard", None),
        P("shard", None),
        P("shard", None),
        P(),
    )
    out_specs = (
        P("shard", None),
        P("shard", None),
        P("shard", None),
        P("group", "shard", None),
        P(),
    )
    return jax.shard_map(
        per_device, mesh=mesh, in_specs=in_specs, out_specs=out_specs, check_vma=False
    )
```

time: 561 us -> 65.9 us (0.12)
  blocking collectives: 263 us -> 0 us
  waiting for transfers between devices: 257 us -> 0 us
  Pallas kernels: 0 us -> 58.5 us
  other arithmetic: 13.6 us -> 0 us
  between operations: 14.1 us -> 0.66 us
  matrix products: 10.3 us -> 0 us
    psum x2 -> x0, blocking collectives: 263 us -> none  [the longest x1 249 us: per_device(): gram = lax.psum(local_gram, 'shard')]
    psum x1 -> x0, waiting for transfers between devices: 257 us -> none  [per_device(): right = lax.psum(term, ('group', 'shard'))]
    pallas_call x0 -> x2, Pallas kernels: none -> 58.5 us  [the longest x1 50.5 us: per_device(): pl.pallas_call(reduce_kernel, out_shape=(jax.ShapeDtypeStruct((ROWS, D),...]
    another operation x5 -> x0, other arithmetic: 12.1 us -> none  [the longest x3 6.52 us: per_device(): chol = jnp.linalg.cholesky(gram)]
    dot_general x4 -> x0, matrix products: 10.2 us -> none  [the longest x1 4.98 us: per_device(): jnp.dot(ortho, new_basis.T, precision=highest, preferred_element_type=jnp...]
  transfers between devices with their start and end apart: 1 -> 0, of which waited for: 1 -> 0; matrix products, arithmetic and copies ran while one was open for 0% -> 0% of each run, Pallas kernels for 0% -> 0%
where the time goes in v1:
time: 65.9 us; the launch traced here: 65.5 us
  Pallas kernels  58.5 us (89%)
  local copies, waits for them, and re-layouts  6.36 us (10%)
  between operations  0.66 us (1%)
    pallas_call x1, Pallas kernels, per_device(): pl.pallas_call(reduce_kernel, out_shape=(jax.ShapeDtypeStruct((ROWS, D),...  50.5 us
    pallas_call x1, Pallas kernels, per_device(): pl.pallas_call(update_kernel, grid=(D // block,), out_shape=[jax.ShapeDty...  7.99 us
    unnamed x12, local copies, waits for them, and re-layouts  6.36 us

profile of v1, /device:TPU:1, one launch (start us, length us, event | category | flops | bytes accessed | tf_op | source)
XLA Modules:
  0.0 65.5 jit_solution(1188248813239981897)
XLA Ops:
  0.6 0.0 copy-start
  0.6 1.3 %copy-done = f32[5120,64]{0,1:T(8,128)S(1)} copy-done((f32[5120,64]{0,1:T(8,128)S(1)}, f32[5120,64]{0,1:T(8,128)}, u32[]{:S(2)}) %copy-start) | copy-done | bytes 1310744
  1.9 0.0 copy-start.2
  2.0 1.2 %copy-done.2 = f32[1,48,5120]{2,1,0:T(8,128)S(1)} copy-done((f32[1,48,5120]{2,1,0:T(8,128)S(1)}, f32[1,48,5120]{2,1,0:T(8,128)}, u32[]{:S(2)}) %copy-start.2) | copy-done | bytes 983064
  3.2 0.0 copy-start.3
  3.2 1.2 %copy-done.3 = f32[1,48,5120]{2,1,0:T(8,128)S(1)} copy-done((f32[1,48,5120]{2,1,0:T(8,128)S(1)}, f32[1,48,5120]{2,1,0:T(8,128)}, u32[]{:S(2)}) %copy-start.3) | copy-done | bytes 983064
  4.4 50.5 %shard_map.101 = (f32[48,5120]{1,0:T(8,128)S(1)}, f32[64,5120]{1,0:T(8,128)S(1)}, f32[112,64]{1,0:T(8,128)S(1)}) custom-call(f32[48,5120]{1,0:T(8,128)S(1)} %bitcast.6, f32[48,5120]{1,0:T(8,128)S(1)} %bitcast.7, f32[64,5120]{1,0:T(8,128)S(1)} %bitcast.5), custom_call_target="tpu_custom_call" | custom-call | tf_op jit(solution)/shard_map/pallas_call | solution.py:277
  54.9 0.0 copy-start.1
  54.9 1.1 %copy-done.1 = f32[64,5120]{1,0:T(8,128)} copy-done((f32[64,5120]{1,0:T(8,128)}, f32[64,5120]{1,0:T(8,128)S(1)}, u32[]{:S(2)}) %copy-start.1) | copy-done | bytes 1310744
  56.0 0.0 copy-start.4
  56.0 1.0 %copy-done.4 = f32[48,5120]{1,0:T(8,128)} copy-done((f32[48,5120]{1,0:T(8,128)}, f32[48,5120]{1,0:T(8,128)S(1)}, u32[]{:S(2)}) %copy-start.4) | copy-done | bytes 983064
  56.9 0.0 copy-start.5
  56.9 0.6 copy-done.5
  57.5 8.0 %shard_map.102 = (f32[48,5120]{1,0:T(8,128)}, f32[48,5120]{1,0:T(8,128)}, f32[48,5120]{1,0:T(8,128)}, f32[48,5120]{1,0:T(8,128)}, f32[64,5120]{1,0:T(8,128)}) custom-call(f32[48,5120]{1,0:T(8,128)} %copy-done.4, f32[64,5120]{1,0:T(8,128)} %copy-done.1, f32[112,64]{1,0:T(8,128)} %copy-done.5, f32[48,5120]{1,0:T(8,128)} %weights.1, f32[48,5120]{1,0:T(8,128)} %momentum.1, ...), custom_call_target="tpu_custom_call" | custom-call | tf_op jit(solution)/shard_map/pallas_call | solution.py:324
Async XLA Ops:
  0.6 1.3 %copy-start = (f32[5120,64]{0,1:T(8,128)S(1)}, f32[5120,64]{0,1:T(8,128)}, u32[]{:S(2)}) copy-start(f32[5120,64]{0,1:T(8,128)} %param.11) | copy-start | bytes 3932164
  1.9 1.2 %copy-start.2 = (f32[1,48,5120]{2,1,0:T(8,128)S(1)}, f32[1,48,5120]{2,1,0:T(8,128)}, u32[]{:S(2)}) copy-start(f32[1,48,5120]{2,1,0:T(8,128)} %param.6) | copy-start | bytes 2949124
  3.2 1.2 %copy-start.3 = (f32[1,48,5120]{2,1,0:T(8,128)S(1)}, f32[1,48,5120]{2,1,0:T(8,128)}, u32[]{:S(2)}) copy-start(f32[1,48,5120]{2,1,0:T(8,128)} %param.7) | copy-start | bytes 2949124
  54.9 1.1 %copy-start.1 = (f32[64,5120]{1,0:T(8,128)}, f32[64,5120]{1,0:T(8,128)S(1)}, u32[]{:S(2)}) copy-start(f32[64,5120]{1,0:T(8,128)S(1)} %get-tuple-element.14.total) | copy-start | bytes 3932164
  56.0 1.0 %copy-start.4 = (f32[48,5120]{1,0:T(8,128)}, f32[48,5120]{1,0:T(8,128)S(1)}, u32[]{:S(2)}) copy-start(f32[48,5120]{1,0:T(8,128)S(1)} %get-tuple-element.13.merged) | copy-start | bytes 2949124
  56.9 0.6 copy-start.5

commit v2 on v1

v2 whole, which is shorter than its diff:
```python
import jax
import jax.numpy as jnp
from jax import lax
from jax.experimental import pallas as pl
from jax.experimental.pallas import tpu as pltpu
from jax.sharding import PartitionSpec as P

MESH = pl.DeviceIdType.MESH
HIGHEST = lax.Precision.HIGHEST
F32 = jnp.float32
BF16 = jnp.bfloat16

outer_rate = 0.7
nesterov_mu = 0.9
anchor_decay = 0.9

D = 5120
RANK = 64
ROWS = 48
NX, NY, NZ = 4, 4, 8
HALF = D // 2
QUARTER = HALF // 4
CHUNKS = ((0, 384), (384, 256))
LOAD = 1280
ZORDER = (4, 3, 5, 2, 6, 1, 7)


def hint(value, multiple):
    return pl.multiple_of(value, multiple)


def dot_nt(a, b):
    return lax.dot_general(a, b, (((1,), (1,)), ((), ())), precision=HIGHEST, preferred_element_type=F32)


def dot(a, b):
    return jnp.dot(a, b, precision=HIGHEST, preferred_element_type=F32)


def split(value):
    high = value.astype(BF16)
    return high, (value - high.astype(F32)).astype(BF16)


def bdot(a, b):
    return jnp.dot(a, b, preferred_element_type=F32)


def eliminate(aug, first, last):
    for j in range(first, last):
        block = j // 8 * 8
        pivot = aug[j : j + 1, j : j + 1]
        scale = lax.rsqrt(pivot)
        scale = scale * (1.5 - 0.5 * pivot * scale * scale)
        row = aug[j : j + 1, :] * scale
        tail = aug[block:, :]
        index = lax.broadcasted_iota(jnp.int32, tail.shape, 0) + block
        moved = tail - (tail[:, j : j + 1] * scale) * row
        tail = jnp.where(index > j, moved, jnp.where(index == j, row, tail))
        aug[block:, :] = tail


def step_kernel(
    delta, error, basis_t, weights, momentum, anchor,
    new_weights, new_momentum, new_anchor, new_error, new_basis,
    d_buf, e_buf, b_buf, w_buf, m_buf, a_buf, merged, total, coef, msib, mst, lbuf, l96, tsend, p1, s1, p2, p3, gfull, gy, gz, gsum, aug,
    load_sem, late_sem, sib_sem, left_sem, p1_sem, p2_sem, p3_sem, p4_sem, p5_sem, fwd_sem, gy_sem, gz_sem, gs_sem,
):
    x = lax.axis_index("group")
    shard = lax.axis_index("shard")
    z = shard // 8
    y = (shard // 2) % 4
    c = shard % 2

    def device(dx, dy, dz, dc):
        return ((x + dx) % NX, ((z + dz) % NZ) * 8 + ((y + dy) % NY) * 2 + (c + dc) % 2)

    def first_axis(d):
        return device(d * (1 - c), d * c, 0, 0)

    def last_axis(d):
        return device(d * c, d * (1 - c), 0, 0)

    sibling = device(0, 0, 0, 1)
    quarter = x * (1 - c) + y * c
    other = y * (1 - c) + x * c

    columns = [hint(((1 - c) * HALF + k * LOAD) % D, 128) for k in range(D // LOAD)]
    loads = []
    for k, col in enumerate(columns):
        cols = pl.ds(col, LOAD)
        group = []
        for j, (src, dst) in enumerate(((delta, d_buf), (error, e_buf), (basis_t, b_buf))):
            copy = pltpu.make_async_copy(src.at[:, cols], dst.at[:, cols], load_sem.at[k, j])
            copy.start()
            group.append(copy)
        loads.append(group)

    barrier = pltpu.get_barrier_semaphore()
    peers = [device(0, 0, d, 0) for d in ZORDER]
    peers += [device(dx, 0, 0, dc) for dc in range(2) for dx in range(NX) if dx or dc]
    peers += [device(0, d, 0, 0) for d in range(1, NY)]
    for peer in peers:
        pl.semaphore_signal(barrier, inc=1, device_id=peer, device_id_type=MESH)

    late = []
    for j, (src, dst) in enumerate(((weights, w_buf), (momentum, m_buf), (anchor, a_buf))):
        copy = pltpu.make_async_copy(src, dst, late_sem.at[j])
        copy.start()
        late.append(copy)

    pending = []

    def send(src, dst, sems, index, peer):
        copy = pltpu.make_async_remote_copy(
            src_ref=src, dst_ref=dst, send_sem=sems.at[(0, *index)], recv_sem=sems.at[(1, *index)],
            device_id=peer, device_id_type=MESH,
        )
        copy.start()
        pending.append(copy)
        return copy

    mine = pl.ds(hint(c * ROWS, 16), ROWS)
    mine_low = pl.ds(hint((2 + c) * ROWS, 16), ROWS)
    theirs = pl.ds(hint((1 - c) * ROWS, 16), ROWS)
    theirs_low = pl.ds(hint((3 - c) * ROWS, 16), ROWS)
    part = jnp.zeros((2 * ROWS, 2 * RANK), F32)
    for k, col in enumerate(columns):
        for copy in loads[k]:
            copy.wait()
        cols = pl.ds(col, LOAD)
        value = d_buf[:, cols] + e_buf[:, cols]
        merged[:, cols] = value
        high, low = split(value)
        if k >= 2:
            mst[mine, (k - 2) * LOAD : (k - 1) * LOAD] = high
            mst[mine_low, (k - 2) * LOAD : (k - 1) * LOAD] = low
        part = part + lax.dot_general(
            jnp.concatenate([high, low], axis=0), jnp.concatenate(split(b_buf[:, cols]), axis=0),
            (((1,), (1,)), ((), ())), preferred_element_type=F32,
        )
    pl.semaphore_wait(barrier, len(peers))
    lane = lax.broadcasted_iota(jnp.int32, (ROWS, 2 * RANK), 1)
    rows_sum = part[:ROWS] + part[ROWS:]
    lbuf[c, x] = jnp.where(lane < RANK, rows_sum + pltpu.roll(rows_sum, RANK, 1), 0.0)

    lefts = []
    for dx, dc in ((2, 0), (2, 1), (1, 0), (3, 0), (1, 1), (3, 1), (0, 1)):
        lefts.append(send(lbuf.at[c, x], lbuf.at[c, x], left_sem, (dc * 4 + dx,), device(dx, 0, 0, dc)))
    away = pl.ds(hint((1 - c) * HALF, 128), HALF)
    moved = send(merged.at[:, away], msib, sib_sem, (0,), sibling)
    moved.wait_recv()
    mst[theirs, :], mst[theirs_low, :] = split(msib[...])
    for copy in lefts:
        copy.wait_recv()
    for core in range(2):
        l96[core * ROWS : (core + 1) * ROWS, :] = (
            (lbuf[core, 0] + lbuf[core, 1]) + lbuf[core, 2]
        ) + lbuf[core, 3]
    left = l96[...]
    left_high = left.astype(BF16).astype(F32)
    pair = left_high + pltpu.roll(left - left_high, RANK, 1)
    left_t = jnp.transpose(jnp.concatenate([pair, pair], axis=0)).astype(BF16)

    first = []
    for n, (off, width) in enumerate(CHUNKS):
        copies = []
        for d in (2, 1, 3, 0):
            start = hint(((quarter + d) % 4) * QUARTER + off, 128)
            term = bdot(left_t, mst[:, pl.ds(start, width)])
            tsend[d, :, off : off + width] = term[:RANK] + term[RANK:]
            if d:
                piece = (d, slice(None), pl.ds(off, width))
                copies.append(send(tsend.at[piece], p1.at[piece], p1_sem, (n, d), first_axis(d)))
        first.append(copies)

    gfull[...] = dot(jnp.transpose(left)[:RANK], left)
    half = pl.ds(hint(c * 32, 32), 32)
    gy[y] = gfull[half, :]
    gram_y = [send(gy.at[y], gy.at[y], gy_sem, (d,), device(0, d, 0, 0)) for d in (2, 1, 3)]

    second = [None] * len(CHUNKS)
    third = [None] * len(CHUNKS)
    fourth = [None] * len(CHUNKS)
    fifth = [None] * len(CHUNKS)
    sixth = [None] * len(CHUNKS)
    base = c * HALF + quarter * QUARTER
    rows = pl.ds(hint(z * 8, 8), 8)

    def scatter_z(n):
        off, width = CHUNKS[n]
        cols = pl.ds(off, width)
        for copy in first[n]:
            copy.wait_recv()
        s1[:, cols] = ((tsend[0, :, cols] + p1[1, :, cols]) + p1[2, :, cols]) + p1[3, :, cols]
        second[n] = []
        for d in ZORDER:
            out = pl.ds(hint(((z + d) % NZ) * 8, 8), 8)
            second[n].append(send(s1.at[out, cols], p2.at[d, :, cols], p2_sem, (n, d), device(0, 0, d, 0)))

    def sum_last(n):
        off, width = CHUNKS[n]
        cols = pl.ds(off, width)
        for copy in second[n]:
            copy.wait_recv()
        value = s1[rows, cols]
        for d in range(1, NZ):
            value = value + p2[d, :, cols]
        p3[other, :, cols] = value
        piece = (other, slice(None), cols)
        third[n] = [send(p3.at[piece], p3.at[piece], p3_sem, (n, d), last_axis(d)) for d in (2, 1, 3)]

    def gather_z(n):
        off, width = CHUNKS[n]
        cols = pl.ds(off, width)
        for copy in third[n]:
            copy.wait_recv()
        place = (rows, pl.ds(hint(base + off, 128), width))
        total[place] = ((p3[0, :, cols] + p3[1, :, cols]) + p3[2, :, cols]) + p3[3, :, cols]
        fourth[n] = [send(total.at[place], total.at[place], p4_sem, (n, d), device(0, 0, d, 0)) for d in ZORDER]

    def gather_first(n):
        off, width = CHUNKS[n]
        for copy in fourth[n]:
            copy.wait_recv()
        place = (slice(None), pl.ds(hint(base + off, 128), width))
        fifth[n] = [(d, send(total.at[place], total.at[place], p5_sem, (n, d), first_axis(d))) for d in (2, 1, 3)]
        sixth[n] = [(0, send(total.at[place], total.at[place], fwd_sem, (n, 0), sibling))]

    def gather_core(n):
        off, width = CHUNKS[n]
        for i in (1, 2, 0):
            d, copy = fifth[n][i]
            copy.wait_recv()
            start = hint(c * HALF + ((quarter + 4 - d) % 4) * QUARTER + off, 128)
            place = (slice(None), pl.ds(start, width))
            sixth[n].append((d, send(total.at[place], total.at[place], fwd_sem, (n, d), sibling)))

    def gram_rest():
        for copy in gram_y:
            copy.wait_recv()
        gz[z] = ((gy[0] + gy[1]) + gy[2]) + gy[3]
        return [send(gz.at[z], gz.at[z], gz_sem, (d,), device(0, 0, d, 0)) for d in ZORDER]

    def gram_swap(copies):
        for copy in copies:
            copy.wait_recv()
        value = gz[0]
        for k in range(1, NZ):
            value = value + gz[k]
        gsum[half, :] = value
        return send(gsum.at[half], gsum.at[half], gs_sem, (0,), sibling)

    def factor():
        lane = lax.broadcasted_iota(jnp.int32, (RANK, 2 * RANK), 1)
        row = lax.broadcasted_iota(jnp.int32, (RANK, 2 * RANK), 0)
        aug[...] = jnp.where(lane < RANK, gsum[...], jnp.where(lane - RANK == row, 1.0, 0.0))
        eliminate(aug, 0, RANK)
        inverse = pltpu.roll(aug[...], RANK, 1)[:, :RANK]
        own = l96[pl.ds(hint(c * ROWS, 8), ROWS), 0:RANK]
        ortho = dot_nt(own, inverse)
        both = 0.25 * jnp.concatenate([inverse, dot(ortho, inverse)], axis=0)
        high, low = split(both)
        coef[...] = jnp.concatenate([high, high, low, low], axis=1)

    def update(start, width):
        cols = pl.ds(start, width)
        high, low = split(total[:, cols])
        both = bdot(coef[...], jnp.concatenate([high, low, high, low], axis=0))
        new_basis[:, cols] = both[:RANK]
        approx = both[RANK:]
        new_error[:, cols] = merged[:, cols] - approx
        speed = nesterov_mu * m_buf[:, cols] + approx
        new_momentum[:, cols] = speed
        stepped = w_buf[:, cols] - outer_rate * (approx + nesterov_mu * speed)
        new_weights[:, cols] = stepped
        new_anchor[:, cols] = anchor_decay * a_buf[:, cols] + (1.0 - anchor_decay) * stepped

    everything = range(len(CHUNKS))
    scatter_z(0)
    gram_z = gram_rest()
    for n in everything[1:]:
        scatter_z(n)
    for n in everything:
        sum_last(n)
    swap = gram_swap(gram_z)
    for n in everything:
        gather_z(n)
    swap.wait_recv()
    factor()
    for copy in late:
        copy.wait()
    for n in everything:
        gather_first(n)
    update(hint(base, 128), QUARTER)
    for n in everything:
        gather_core(n)
    for d in (1, 3, 2):
        update(hint(c * HALF + ((quarter + 4 - d) % 4) * QUARTER, 128), QUARTER)
    there = y * (1 - c) + x * c
    for d in (0, 1, 3, 2):
        for n in everything:
            for key, copy in sixth[n]:
                if key == d:
                    copy.wait_recv()
        update(hint((1 - c) * HALF + ((there + 4 - d) % 4) * QUARTER, 128), QUARTER)

    for copy in pending:
        copy.wait_send()


def store_kernel(*refs):
    sems = refs[-1]
    count = len(refs) // 2
    copies = [pltpu.make_async_copy(refs[k], refs[count + k], sems.at[k]) for k in range(count)]
    for copy in copies:
        copy.start()
    for copy in copies:
        copy.wait()


def per_device(delta, error, weights, momentum, anchor, basis):
    count = len(CHUNKS)
    hbm = pl.BlockSpec(memory_space=pltpu.HBM)
    vmem = pl.BlockSpec(memory_space=pltpu.VMEM)
    dma = pltpu.SemaphoreType.DMA
    shapes = [jax.ShapeDtypeStruct((ROWS, D), F32)] * 4 + [jax.ShapeDtypeStruct((RANK, D), F32)]
    outs = pl.pallas_call(
        step_kernel,
        out_shape=shapes,
        in_specs=[hbm] * 6,
        out_specs=[vmem] * 5,
        scratch_shapes=[
            pltpu.VMEM((ROWS, D), F32),
            pltpu.VMEM((ROWS, D), F32),
            pltpu.VMEM((RANK, D), F32),
            pltpu.VMEM((ROWS, D), F32),
            pltpu.VMEM((ROWS, D), F32),
            pltpu.VMEM((ROWS, D), F32),
            pltpu.VMEM((ROWS, D), F32),
            pltpu.VMEM((RANK, D), F32),
            pltpu.VMEM((RANK + ROWS, 4 * RANK), BF16),
            pltpu.VMEM((ROWS, HALF), F32),
            pltpu.VMEM((4 * ROWS, HALF), BF16),
            pltpu.VMEM((2, NX, ROWS, 2 * RANK), F32),
            pltpu.VMEM((2 * ROWS, 2 * RANK), F32),
            pltpu.VMEM((4, RANK, QUARTER), F32),
            pltpu.VMEM((4, RANK, QUARTER), F32),
            pltpu.VMEM((RANK, QUARTER), F32),
            pltpu.VMEM((NZ, 8, QUARTER), F32),
            pltpu.VMEM((4, 8, QUARTER), F32),
            pltpu.VMEM((RANK, 2 * RANK), F32),
            pltpu.VMEM((NY, 32, 2 * RANK), F32),
            pltpu.VMEM((NZ, 32, 2 * RANK), F32),
            pltpu.VMEM((RANK, 2 * RANK), F32),
            pltpu.VMEM((RANK, 2 * RANK), F32),
            dma((D // LOAD, 3)),
            dma((3,)),
            dma((2, 1)),
            dma((2, 8)),
            dma((2, count, 4)),
            dma((2, count, 8)),
            dma((2, count, 4)),
            dma((2, count, 8)),
            dma((2, count, 4)),
            dma((2, count, 4)),
            dma((2, 4)),
            dma((2, 8)),
            dma((2, 1)),
        ],
        compiler_params=pltpu.CompilerParams(collective_id=0, has_side_effects=True, vmem_limit_bytes=32 << 20),
    )(*(pltpu.with_memory_space_constraint(a, pltpu.HBM) for a in (delta[0], error[0], basis.T, weights, momentum, anchor)))
    outs = pl.pallas_call(
        store_kernel,
        out_shape=shapes,
        in_specs=[vmem] * 5,
        out_specs=[hbm] * 5,
        scratch_shapes=[dma((5,))],
        compiler_params=pltpu.CompilerParams(vmem_limit_bytes=1 << 20),
    )(*(pltpu.with_memory_space_constraint(a, pltpu.VMEM) for a in outs))
    new_weights, new_momentum, new_anchor, new_error, new_basis = outs
    return (new_weights, new_momentum, new_anchor, new_error[None], new_basis.T)


def solution(mesh):
    in_specs = (
        P("group", "shard", None),
        P("group", "shard", None),
        P("shard", None),
        P("shard", None),
        P("shard", None),
        P(),
    )
    out_specs = (
        P("shard", None),
        P("shard", None),
        P("shard", None),
        P("group", "shard", None),
        P(),
    )
    return jax.shard_map(
        per_device, mesh=mesh, in_specs=in_specs, out_specs=out_specs, check_vma=False
    )
```

time: 65.9 us -> 52.3 us (0.79)
  Pallas kernels: 58.5 us -> 51.6 us
  local copies, waits for them, and re-layouts: 6.36 us -> 0 us
    pallas_call x2, Pallas kernels: 58.5 us -> 51.6 us  [the longest x1 49.2 us: per_device(): pl.pallas_call(step_kernel, out_shape=shapes, in_specs=[hbm] * 6, out_spe...]
    unnamed x12 -> x0, local copies, waits for them, and re-layouts: 6.36 us -> none
where the time goes in v2:
time: 52.3 us; the launch traced here: 52.2 us
  Pallas kernels  51.6 us (99%)
  between operations  0.64 us (1%)
    pallas_call x1, Pallas kernels, per_device(): pl.pallas_call(step_kernel, out_shape=shapes, in_specs=[hbm] * 6, out_spe...  49.2 us
    pallas_call x1, Pallas kernels, per_device(): pl.pallas_call(store_kernel, out_shape=shapes, in_specs=[vmem] * 5, out_s...  2.4 us

profile of v2, /device:TPU:1, one launch (start us, length us, event | category | flops | bytes accessed | tf_op | source)
XLA Modules:
  0.0 52.2 jit_solution(10449384099775410857)
XLA Ops:
  0.6 49.2 %shard_map.101 = (f32[48,5120]{1,0:T(8,128)S(1)}, f32[48,5120]{1,0:T(8,128)S(1)}, f32[48,5120]{1,0:T(8,128)S(1)}, f32[48,5120]{1,0:T(8,128)S(1)}, f32[64,5120]{1,0:T(8,128)S(1)}) custom-call(f32[48,5120]{1,0:T(8,128)} %bitcast.6, f32[48,5120]{1,0:T(8,128)} %bitcast.7, f32[64,5120]{1,0:T(8,128)} %bitcast.5, f32[48,5120]{1,0:T(8,128)} %weights.1, ...), custom_call_target="tpu_custom_call" | custom-call | tf_op jit(solution)/shard_map/pallas_call | solution.py:328
  49.8 2.4 %shard_map.102 = (f32[48,5120]{1,0:T(8,128)}, f32[48,5120]{1,0:T(8,128)}, f32[48,5120]{1,0:T(8,128)}, f32[48,5120]{1,0:T(8,128)}, f32[64,5120]{1,0:T(8,128)}) custom-call(f32[48,5120]{1,0:T(8,128)S(1)} %get-tuple-element.15.refs_0_, f32[48,5120]{1,0:T(8,128)S(1)} %get-tuple-element.16.refs_1_, f32[48,5120]{1,0:T(8,128)S(1)} %get-tuple-element.17.refs_2_, ...), custom_call_target="tpu_custom_call" | custom-call | tf_op jit(solution)/shard_map/pallas_call | solution.py:373

commit v3 on v2

v3 whole, which is shorter than its diff:
```python
import jax
import jax.numpy as jnp
from jax import lax
from jax.experimental import pallas as pl
from jax.experimental.pallas import tpu as pltpu
from jax.sharding import PartitionSpec as P

MESH = pl.DeviceIdType.MESH
HIGHEST = lax.Precision.HIGHEST
F32 = jnp.float32
BF16 = jnp.bfloat16

outer_rate = 0.7
nesterov_mu = 0.9
anchor_decay = 0.9

D = 5120
RANK = 64
ROWS = 48
NX, NY, NZ = 4, 4, 8
HALF = D // 2
PLANE = 896
ZFIRST = HALF - 2 * PLANE
CHUNKS = ((True, 0, 384), (False, 0, 512), (True, 384, 384), (False, 512, 384))
LOAD = 1280
ZORDER = (4, 3, 5, 2, 6, 1, 7)
PLANEORDER = ((2, 0), (2, 1), (1, 0), (3, 0), (1, 1), (3, 1), (0, 1))
XYORDER = ((2, 2), (2, 1), (2, 3), (1, 2), (3, 2), (2, 0), (0, 2), (1, 1), (1, 3), (3, 1), (3, 3), (1, 0), (3, 0), (0, 1), (0, 3))


def hint(value, multiple):
    return pl.multiple_of(value, multiple)


def dot_nt(a, b):
    return lax.dot_general(a, b, (((1,), (1,)), ((), ())), precision=HIGHEST, preferred_element_type=F32)


def dot(a, b):
    return jnp.dot(a, b, precision=HIGHEST, preferred_element_type=F32)


def split(value):
    high = value.astype(BF16)
    return high, (value - high.astype(F32)).astype(BF16)


def bdot(a, b):
    return jnp.dot(a, b, preferred_element_type=F32)


def eliminate(blocks, first, last):
    index = lax.broadcasted_iota(jnp.int32, (8, 1), 0)
    for j in range(first, last):
        own = j // 8
        row = blocks[own][j % 8 : j % 8 + 1, :]
        row = row * (1.0 / row[:, j : j + 1])
        for k in range(own, RANK // 8):
            column = blocks[k][:, j : j + 1]
            if k == own:
                column = jnp.where(index > j % 8, column, 0.0)
            blocks[k] = blocks[k] - column * row
    return blocks


def step_kernel(
    delta, error, basis_t, weights, momentum, anchor,
    new_weights, new_momentum, new_anchor, new_error, new_basis,
    d_buf, e_buf, b_buf, w_buf, m_buf, a_buf, merged, total, coef, msib, mst, lbuf, l96, term, ra1, rc1, ra2, rc2, gfull, gy, gz, gx,
    load_sem, late_sem, sib_sem, left_sem, sem1, sem2, sem3, fwd_sem, gram_sem,
):
    x = lax.axis_index("group")
    shard = lax.axis_index("shard")
    z = lax.div(shard, 8)
    y = lax.rem(lax.div(shard, 2), 4)
    c = lax.rem(shard, 2)
    plane = x * NY + y

    xs = [lax.rem(x + d, NX) for d in range(NX)]
    ys = [lax.rem(y + d, NY) for d in range(NY)]
    zs = [lax.rem(z + d, NZ) for d in range(NZ)]
    cs = [c, 1 - c]
    known = {}

    def device(dx, dy, dz, dc):
        key = (dx, dy, dz, dc)
        if key not in known:
            known[key] = (xs[dx], zs[dz] * 8 + ys[dy] * 2 + cs[dc])
        return known[key]

    sibling = device(0, 0, 0, 1)

    barrier = pltpu.get_barrier_semaphore()
    peers = [device(0, 0, d, 0) for d in ZORDER]
    peers += [device(dx, dy, 0, 0) for dx, dy in XYORDER]
    peers += [device(dx, 0, 0, 1) for dx in (2, 1, 3, 0)]
    for peer in peers:
        pl.semaphore_signal(barrier, inc=1, device_id=peer, device_id_type=MESH)

    columns = [hint(((1 - c) * HALF + k * LOAD) % D, 128) for k in range(D // LOAD)]
    loads = []
    for k, col in enumerate(columns):
        cols = pl.ds(col, LOAD)
        group = []
        for j, (src, dst) in enumerate(((delta, d_buf), (error, e_buf), (basis_t, b_buf))):
            copy = pltpu.make_async_copy(src.at[:, cols], dst.at[:, cols], load_sem.at[k, j])
            copy.start()
            group.append(copy)
        loads.append(group)

    late = []
    for j, (src, dst) in enumerate(((weights, w_buf), (momentum, m_buf), (anchor, a_buf))):
        copy = pltpu.make_async_copy(src, dst, late_sem.at[j])
        copy.start()
        late.append(copy)

    pending = []

    def link(src, dst, sems, n, peer):
        return pltpu.make_async_remote_copy(
            src_ref=src, dst_ref=dst, send_sem=sems.at[0, n], recv_sem=sems.at[1, n],
            device_id=peer, device_id_type=MESH,
        )

    def send_all(pieces, sems, n, like):
        for src, dst, peer in pieces:
            link(src, dst, sems, n, peer).start()
        copy = link(like, like, sems, n, sibling)
        pending.append(copy)
        return copy

    mine = pl.ds(hint(c * ROWS, 16), ROWS)
    mine_low = pl.ds(hint((2 + c) * ROWS, 16), ROWS)
    theirs = pl.ds(hint((1 - c) * ROWS, 16), ROWS)
    theirs_low = pl.ds(hint((3 - c) * ROWS, 16), ROWS)
    part = jnp.zeros((2 * ROWS, 2 * RANK), F32)
    for k, col in enumerate(columns):
        for copy in loads[k]:
            copy.wait()
        cols = pl.ds(col, LOAD)
        value = d_buf[:, cols] + e_buf[:, cols]
        merged[:, cols] = value
        high, low = split(value)
        if k >= 2:
            mst[mine, (k - 2) * LOAD : (k - 1) * LOAD] = high
            mst[mine_low, (k - 2) * LOAD : (k - 1) * LOAD] = low
        part = part + lax.dot_general(
            jnp.concatenate([high, low], axis=0), jnp.concatenate(split(b_buf[:, cols]), axis=0),
            (((1,), (1,)), ((), ())), preferred_element_type=F32,
        )
    pl.semaphore_wait(barrier, len(peers))
    part = part[:ROWS] + part[ROWS:]
    part = part + pltpu.roll(part, RANK, 1)
    low_lanes = lax.broadcasted_iota(jnp.int32, (ROWS // 2, 2 * RANK), 1) < RANK
    lbuf[c * NX + x] = jnp.where(low_lanes, part[: ROWS // 2], part[ROWS // 2 :])

    slot = lbuf.at[c * NX + x]
    lefts = send_all([(slot, slot, device(dx, 0, 0, dc)) for dx, dc in PLANEORDER], left_sem, 0, lbuf.at[0:7])
    away = merged.at[:, pl.ds(hint((1 - c) * HALF, 128), HALF)]
    moved = send_all([(away, msib, sibling)], sib_sem, 0, msib)
    moved.wait_recv()
    mst[theirs, :], mst[theirs_low, :] = split(msib[...])
    lefts.wait_recv()
    for core in range(2):
        packed = ((lbuf[core * NX] + lbuf[core * NX + 1]) + lbuf[core * NX + 2]) + lbuf[core * NX + 3]
        l96[core * ROWS : core * ROWS + ROWS // 2, :] = jnp.where(low_lanes, packed, 0.0)
        l96[core * ROWS + ROWS // 2 : (core + 1) * ROWS, :] = jnp.where(low_lanes, pltpu.roll(packed, RANK, 1), 0.0)
    left = l96[...]
    left_high = left.astype(BF16).astype(F32)
    pair = left_high + pltpu.roll(left - left_high, RANK, 1)
    left_t = jnp.transpose(jnp.concatenate([pair, pair], axis=0)).astype(BF16)

    def terms(start, width):
        value = bdot(left_t, mst[:, start : start + width])
        term[:, start : start + width] = value[:RANK] + value[RANK:]

    count = len(CHUNKS)
    z_rows = pl.ds(hint(z * 8, 8), 8)
    plane_rows = pl.ds(hint(lax.div(plane, 2) * 8, 8), 8)
    plane_col = lax.rem(plane, 2) * PLANE
    out_rows = [pl.ds(hint(zs[d] * 8, 8), 8) for d in range(NZ)]
    out_plane = {}
    for dx, dy in XYORDER:
        piece = xs[dx] * NY + ys[dy]
        out_plane[dx, dy] = (pl.ds(hint(lax.div(piece, 2) * 8, 8), 8), lax.rem(piece, 2) * PLANE)

    def over_z(src, dst, sems, n, like):
        return send_all([(src, dst, device(0, 0, d, 0)) for d in ZORDER], sems, n, like)

    def over_xy(src, dst, sems, n, like):
        return send_all([(src, dst, device(dx, dy, 0, 0)) for dx, dy in XYORDER], sems, n, like)

    def stage0(n):
        zfirst, off, width = CHUNKS[n]
        cols = pl.ds(off, width)
        if zfirst:
            start = 2 * PLANE + off
            terms(start, width)
            pieces = [(term.at[out_rows[d], pl.ds(start, width)], rc1.at[d, :, cols], device(0, 0, d, 0)) for d in ZORDER]
            return send_all(pieces, sem1, n, rc1.at[1:NZ, :, cols])
        for side in range(2):
            terms(side * PLANE + off, width)
        pieces = []
        for dx, dy in XYORDER:
            rows, col = out_plane[dx, dy]
            src = term.at[rows, pl.ds(hint(col + off, 128), width)]
            pieces.append((src, ra1.at[dx * NY + dy, :, cols], device(dx, dy, 0, 0)))
        return send_all(pieces, sem1, n, ra1.at[1 : NX * NY, :, cols])

    def stage1(n):
        zfirst, off, width = CHUNKS[n]
        cols = pl.ds(off, width)
        first[n].wait_recv()
        if zfirst:
            value = term[z_rows, pl.ds(2 * PLANE + off, width)]
            for d in range(1, NZ):
                value = value + rc1[d, :, cols]
            rc2[plane, :, cols] = value
            piece = rc2.at[plane, :, cols]
            return over_xy(piece, piece, sem2, n, rc2.at[1 : NX * NY, :, cols])
        value = term[plane_rows, pl.ds(hint(plane_col + off, 128), width)]
        for d in range(1, NX * NY):
            value = value + ra1[d, :, cols]
        ra2[z, :, cols] = value
        piece = ra2.at[z, :, cols]
        return over_z(piece, piece, sem2, n, ra2.at[1:NZ, :, cols])

    def stage2(n):
        zfirst, off, width = CHUNKS[n]
        cols = pl.ds(off, width)
        second[n].wait_recv()
        if zfirst:
            value = rc2[0, :, cols]
            for k in range(1, NX * NY):
                value = value + rc2[k, :, cols]
            place = (z_rows, pl.ds(hint(c * HALF + 2 * PLANE + off, 128), width))
            total[place] = value
            return over_z(total.at[place], total.at[place], sem3, n, rc1.at[1:NZ, :, cols])
        value = ra2[0, :, cols]
        for k in range(1, NZ):
            value = value + ra2[k, :, cols]
        place = (plane_rows, pl.ds(hint(c * HALF + plane_col + off, 128), width))
        total[place] = value
        return over_xy(total.at[place], total.at[place], sem3, n, ra1.at[1 : NX * NY, :, cols])

    def ranges(n, core):
        zfirst, off, width = CHUNKS[n]
        starts = (2 * PLANE + off,) if zfirst else (off, PLANE + off)
        return [pl.ds(hint(core * HALF + start, 128), width) for start in starts]

    def stage3(n):
        third[n].wait_recv()
        places = [total.at[:, cols] for cols in ranges(n, c)]
        return send_all([(p, p, sibling) for p in places], fwd_sem, n, term.at[:, 0 : len(places) * CHUNKS[n][2]])

    share = x * 2 + c

    def gram_start():
        gfull[...] = dot(jnp.transpose(left)[:RANK], left)
        gy[y] = gfull[pl.ds(hint(share * 8, 8), 8), :]
        pieces = [(gy.at[y], gy.at[y], device(0, d, 0, 0)) for d in (2, 1, 3)]
        return send_all(pieces, gram_sem, 0, gy.at[1:NY])

    def gram_middle(copies):
        copies.wait_recv()
        gz[z] = ((gy[0] + gy[1]) + gy[2]) + gy[3]
        return over_z(gz.at[z], gz.at[z], gram_sem, 1, gz.at[1:NZ])

    def gram_end(copies):
        copies.wait_recv()
        value = gz[0]
        for k in range(1, NZ):
            value = value + gz[k]
        gx[share] = value
        pieces = [(gx.at[share], gx.at[share], device(dx, 0, 0, dc)) for dx, dc in PLANEORDER]
        return send_all(pieces, gram_sem, 2, gx.at[1:8])

    def gram_blocks():
        lane = lax.broadcasted_iota(jnp.int32, (8, 2 * RANK), 1)
        row = lax.broadcasted_iota(jnp.int32, (8, 2 * RANK), 0)
        return [
            jnp.where(lane < RANK, gx[k], jnp.where(lane == row + (RANK + 8 * k), 1.0, 0.0)) for k in range(RANK // 8)
        ]

    def coefficients(blocks):
        whole = jnp.concatenate(blocks, axis=0)
        lane = lax.broadcasted_iota(jnp.int32, (RANK, 2 * RANK), 1)
        row = lax.broadcasted_iota(jnp.int32, (RANK, 2 * RANK), 0)
        pivot = jnp.sum(jnp.where(lane == row, whole, 0.0), axis=1, keepdims=True)
        scale = lax.rsqrt(pivot)
        scale = scale * (1.5 - 0.5 * pivot * scale * scale)
        inverse = (pltpu.roll(whole, RANK, 1) * scale)[:, :RANK]
        own = l96[pl.ds(hint(c * ROWS, 8), ROWS), 0:RANK]
        ortho = dot_nt(own, inverse)
        both = 0.25 * jnp.concatenate([inverse, dot(ortho, inverse)], axis=0)
        high, low = split(both)
        coef[...] = jnp.concatenate([high, high, low, low], axis=1)

    def update(cols):
        high, low = split(total[:, cols])
        both = bdot(coef[...], jnp.concatenate([high, low, high, low], axis=0))
        new_basis[:, cols] = both[:RANK]
        approx = both[RANK:]
        new_error[:, cols] = merged[:, cols] - approx
        speed = nesterov_mu * m_buf[:, cols] + approx
        new_momentum[:, cols] = speed
        stepped = w_buf[:, cols] - outer_rate * (approx + nesterov_mu * speed)
        new_weights[:, cols] = stepped
        new_anchor[:, cols] = anchor_decay * a_buf[:, cols] + (1.0 - anchor_decay) * stepped

    def update_own(n):
        for cols in ranges(n, c):
            update(cols)

    def update_sibling(n):
        fourth[n].wait_recv()
        for cols in ranges(n, 1 - c):
            update(cols)

    early = count // 2
    first = [stage0(n) for n in range(early)]
    gram = gram_start()
    first += [stage0(n) for n in range(early, count)]
    gram = gram_middle(gram)
    second = [stage1(n) for n in range(early)]
    gram = gram_end(gram)
    second += [stage1(n) for n in range(early, count)]
    gram.wait_recv()
    blocks = eliminate(gram_blocks(), 0, 32)
    third = [stage2(n) for n in range(count)]
    coefficients(eliminate(blocks, 32, RANK))
    for copy in late:
        copy.wait()
    fourth = []
    for n in range(count):
        fourth.append(stage3(n))
        if n:
            update_own(n - 1)
    for n in range(count - 1):
        update_sibling(n)
    update_own(count - 1)
    update_sibling(count - 1)
    for copy in pending:
        copy.wait_send()


def store_kernel(*refs):
    sems = refs[-1]
    count = len(refs) // 2
    copies = [pltpu.make_async_copy(refs[k], refs[count + k], sems.at[k]) for k in range(count)]
    for copy in copies:
        copy.start()
    for copy in copies:
        copy.wait()


def per_device(delta, error, weights, momentum, anchor, basis):
    count = len(CHUNKS)
    hbm = pl.BlockSpec(memory_space=pltpu.HBM)
    vmem = pl.BlockSpec(memory_space=pltpu.VMEM)
    dma = pltpu.SemaphoreType.DMA
    shapes = [jax.ShapeDtypeStruct((ROWS, D), F32)] * 4 + [jax.ShapeDtypeStruct((RANK, D), F32)]
    outs = pl.pallas_call(
        step_kernel,
        out_shape=shapes,
        in_specs=[hbm] * 6,
        out_specs=[vmem] * 5,
        scratch_shapes=[
            pltpu.VMEM((ROWS, D), F32),
            pltpu.VMEM((ROWS, D), F32),
            pltpu.VMEM((RANK, D), F32),
            pltpu.VMEM((ROWS, D), F32),
            pltpu.VMEM((ROWS, D), F32),
            pltpu.VMEM((ROWS, D), F32),
            pltpu.VMEM((ROWS, D), F32),
            pltpu.VMEM((RANK, D), F32),
            pltpu.VMEM((RANK + ROWS, 4 * RANK), BF16),
            pltpu.VMEM((ROWS, HALF), F32),
            pltpu.VMEM((4 * ROWS, HALF), BF16),
            pltpu.VMEM((2 * NX, ROWS // 2, 2 * RANK), F32),
            pltpu.VMEM((2 * ROWS, 2 * RANK), F32),
            pltpu.VMEM((RANK, HALF), F32),
            pltpu.VMEM((NX * NY, 8, PLANE), F32),
            pltpu.VMEM((NZ, 8, ZFIRST), F32),
            pltpu.VMEM((NZ, 8, PLANE), F32),
            pltpu.VMEM((NX * NY, 8, ZFIRST), F32),
            pltpu.VMEM((RANK, 2 * RANK), F32),
            pltpu.VMEM((NY, 8, 2 * RANK), F32),
            pltpu.VMEM((NZ, 8, 2 * RANK), F32),
            pltpu.VMEM((8, 8, 2 * RANK), F32),
            dma((D // LOAD, 3)),
            dma((3,)),
            dma((2, 1)),
            dma((2, 1)),
            dma((2, count)),
            dma((2, count)),
            dma((2, count)),
            dma((2, count)),
            dma((2, 3)),
        ],
        compiler_params=pltpu.CompilerParams(collective_id=0, has_side_effects=True, vmem_limit_bytes=32 << 20),
    )(*(pltpu.with_memory_space_constraint(a, pltpu.HBM) for a in (delta[0], error[0], basis.T, weights, momentum, anchor)))
    outs = pl.pallas_call(
        store_kernel,
        out_shape=shapes,
        in_specs=[vmem] * 5,
        out_specs=[hbm] * 5,
        scratch_shapes=[dma((5,))],
        compiler_params=pltpu.CompilerParams(vmem_limit_bytes=1 << 20),
    )(*(pltpu.with_memory_space_constraint(a, pltpu.VMEM) for a in outs))
    new_weights, new_momentum, new_anchor, new_error, new_basis = outs
    return (new_weights, new_momentum, new_anchor, new_error[None], new_basis.T)


def solution(mesh):
    in_specs = (
        P("group", "shard", None),
        P("group", "shard", None),
        P("shard", None),
        P("shard", None),
        P("shard", None),
        P(),
    )
    out_specs = (
        P("shard", None),
        P("shard", None),
        P("shard", None),
        P("group", "shard", None),
        P(),
    )
    return jax.shard_map(
        per_device, mesh=mesh, in_specs=in_specs, out_specs=out_specs, check_vma=False
    )
```

time: 52.3 us -> 46.9 us (0.90)
  Pallas kernels: 51.6 us -> 46.2 us
    pallas_call x1, Pallas kernels: 49.2 us -> 43.8 us  [per_device(): pl.pallas_call(step_kernel, out_shape=shapes, in_specs=[hbm] * 6, out_spe...]
where the time goes in v3:
time: 46.9 us; the launch traced here: 46.8 us
  Pallas kernels  46.2 us (99%)
  between operations  0.64 us (1%)
    pallas_call x1, Pallas kernels, per_device(): pl.pallas_call(step_kernel, out_shape=shapes, in_specs=[hbm] * 6, out_spe...  43.8 us
    pallas_call x1, Pallas kernels, per_device(): pl.pallas_call(store_kernel, out_shape=shapes, in_specs=[vmem] * 5, out_s...  2.4 us

profile of v3, /device:TPU:1, one launch (start us, length us, event | category | flops | bytes accessed | tf_op | source)
XLA Modules:
  0.0 46.8 jit_solution(14472611825207878160)
XLA Ops:
  0.6 43.8 %shard_map.101 = (f32[48,5120]{1,0:T(8,128)S(1)}, f32[48,5120]{1,0:T(8,128)S(1)}, f32[48,5120]{1,0:T(8,128)S(1)}, f32[48,5120]{1,0:T(8,128)S(1)}, f32[64,5120]{1,0:T(8,128)S(1)}) custom-call(f32[48,5120]{1,0:T(8,128)} %bitcast.6, f32[48,5120]{1,0:T(8,128)} %bitcast.7, f32[64,5120]{1,0:T(8,128)} %bitcast.5, f32[48,5120]{1,0:T(8,128)} %weights.1, ...), custom_call_target="tpu_custom_call" | custom-call | tf_op jit(solution)/shard_map/pallas_call | solution.py:363
  44.4 2.4 %shard_map.102 = (f32[48,5120]{1,0:T(8,128)}, f32[48,5120]{1,0:T(8,128)}, f32[48,5120]{1,0:T(8,128)}, f32[48,5120]{1,0:T(8,128)}, f32[64,5120]{1,0:T(8,128)}) custom-call(f32[48,5120]{1,0:T(8,128)S(1)} %get-tuple-element.15.refs_0_, f32[48,5120]{1,0:T(8,128)S(1)} %get-tuple-element.16.refs_1_, f32[48,5120]{1,0:T(8,128)S(1)} %get-tuple-element.17.refs_2_, ...), custom_call_target="tpu_custom_call" | custom-call | tf_op jit(solution)/shard_map/pallas_call | solution.py:403

commit v4 on v3

--- a/solution.py
+++ b/solution.py
@@ -23,6 +23,7 @@
 ZFIRST = HALF - 2 * PLANE
 CHUNKS = ((True, 0, 384), (False, 0, 512), (True, 384, 384), (False, 512, 384))
 LOAD = 1280
+GROUP = 4
 ZORDER = (4, 3, 5, 2, 6, 1, 7)
 PLANEORDER = ((2, 0), (2, 1), (1, 0), (3, 0), (1, 1), (3, 1), (0, 1))
 XYORDER = ((2, 2), (2, 1), (2, 3), (1, 2), (3, 2), (2, 0), (0, 2), (1, 1), (1, 3), (3, 1), (3, 3), (1, 0), (3, 0), (0, 1), (0, 3))
@@ -51,15 +52,38 @@
 
 def eliminate(blocks, first, last):
     index = lax.broadcasted_iota(jnp.int32, (8, 1), 0)
-    for j in range(first, last):
-        own = j // 8
-        row = blocks[own][j % 8 : j % 8 + 1, :]
-        row = row * (1.0 / row[:, j : j + 1])
+    for j in range(first, last, GROUP):
+        own, at = j // 8, j % 8
+        steps = range(GROUP)
+        columns = {
+            (k, t): jnp.broadcast_to(blocks[k][:, j + t : j + t + 1], (8, 2 * RANK))
+            for k in range(own, RANK // 8) for t in steps
+        }
+        rows = [blocks[own][at + t : at + t + 1, :] for t in steps]
+        small = {(i, t): columns[own, t][at + i : at + i + 1, :] for i in steps for t in steps}
+        unit, ratio = [], {}
+        for t in steps:
+            inverse = 1.0 / small[t, t]
+            unit.append(rows[t] * inverse)
+            for i in range(t + 1, GROUP):
+                ratio[t, i] = small[t, i] * inverse
+            for i in range(t + 1, GROUP):
+                rows[i] = rows[i] - small[i, t] * unit[t]
+                for k in range(t + 1, GROUP):
+                    small[i, k] = small[i, k] - small[i, t] * ratio[t, k]
         for k in range(own, RANK // 8):
-            column = blocks[k][:, j : j + 1]
+            value, done = blocks[k], []
+            for t in steps:
+                column = columns[k, t]
+                for i in range(t):
+                    column = column - done[i] * ratio[i, t]
+                done.append(column)
+                value = value - column * unit[t]
             if k == own:
-                column = jnp.where(index > j % 8, column, 0.0)
-            blocks[k] = blocks[k] - column * row
+                value = jnp.where(index >= at + GROUP, value, blocks[k])
+                for t in steps:
+                    value = jnp.where(index == at + t, rows[t], value)
+            blocks[k] = value
     return blocks
 
 
@@ -318,16 +342,20 @@
             update(cols)
 
     early = count // 2
-    first = [stage0(n) for n in range(early)]
+    first = [stage0(0)]
     gram = gram_start()
-    first += [stage0(n) for n in range(early, count)]
+    first += [stage0(n) for n in range(1, count)]
     gram = gram_middle(gram)
     second = [stage1(n) for n in range(early)]
     gram = gram_end(gram)
     second += [stage1(n) for n in range(early, count)]
+    third = [stage2(n) for n in range(early)]
     gram.wait_recv()
-    blocks = eliminate(gram_blocks(), 0, 32)
-    third = [stage2(n) for n in range(count)]
+    blocks = eliminate(gram_blocks(), 0, 16)
+    for n in range(early, count):
+        third.append(stage2(n))
+        if n < count - 1:
+            blocks = eliminate(blocks, 16, 32)
     coefficients(eliminate(blocks, 32, RANK))
     for copy in late:
         copy.wait()

time: 46.9 us -> 40.7 us (0.87)
  Pallas kernels: 46.2 us -> 40 us
    pallas_call x1, Pallas kernels: 43.8 us -> 37.6 us  [per_device(): pl.pallas_call(step_kernel, out_shape=shapes, in_specs=[hbm] * 6, out_spe...]
where the time goes in v4:
time: 40.7 us
  Pallas kernels  40 us (98%)
  between operations  0.64 us (2%)
    pallas_call x1, Pallas kernels, per_device(): pl.pallas_call(step_kernel, out_shape=shapes, in_specs=[hbm] * 6, out_spe...  37.6 us
    pallas_call x1, Pallas kernels, per_device(): pl.pallas_call(store_kernel, out_shape=shapes, in_specs=[vmem] * 5, out_s...  2.4 us

profile of v4, /device:TPU:1, one launch (start us, length us, event | category | flops | bytes accessed | tf_op | source)
XLA Modules:
  0.0 40.7 jit_solution(425692694024276678)
XLA Ops:
  0.6 37.6 %shard_map.101 = (f32[48,5120]{1,0:T(8,128)S(1)}, f32[48,5120]{1,0:T(8,128)S(1)}, f32[48,5120]{1,0:T(8,128)S(1)}, f32[48,5120]{1,0:T(8,128)S(1)}, f32[64,5120]{1,0:T(8,128)S(1)}) custom-call(f32[48,5120]{1,0:T(8,128)} %bitcast.6, f32[48,5120]{1,0:T(8,128)} %bitcast.7, f32[64,5120]{1,0:T(8,128)} %bitcast.5, f32[48,5120]{1,0:T(8,128)} %weights.1, ...), custom_call_target="tpu_custom_call" | custom-call | tf_op jit(solution)/shard_map/pallas_call | solution.py:391
  38.3 2.4 %shard_map.102 = (f32[48,5120]{1,0:T(8,128)}, f32[48,5120]{1,0:T(8,128)}, f32[48,5120]{1,0:T(8,128)}, f32[48,5120]{1,0:T(8,128)}, f32[64,5120]{1,0:T(8,128)}) custom-call(f32[48,5120]{1,0:T(8,128)S(1)} %get-tuple-element.15.refs_0_, f32[48,5120]{1,0:T(8,128)S(1)} %get-tuple-element.16.refs_1_, f32[48,5120]{1,0:T(8,128)S(1)} %get-tuple-element.17.refs_2_, ...), custom_call_target="tpu_custom_call" | custom-call | tf_op jit(solution)/shard_map/pallas_call | solution.py:431

commit v5 on v4

--- a/solution.py
+++ b/solution.py
@@ -21,7 +21,7 @@
 HALF = D // 2
 PLANE = 896
 ZFIRST = HALF - 2 * PLANE
-CHUNKS = ((True, 0, 384), (False, 0, 512), (True, 384, 384), (False, 512, 384))
+CHUNKS = ((True, 0, 256), (False, 0, 384), (True, 256, 256), (False, 384, 256), (True, 512, 256), (False, 640, 256))
 LOAD = 1280
 GROUP = 4
 ZORDER = (4, 3, 5, 2, 6, 1, 7)
@@ -172,12 +172,12 @@
             jnp.concatenate([high, low], axis=0), jnp.concatenate(split(b_buf[:, cols]), axis=0),
             (((1,), (1,)), ((), ())), preferred_element_type=F32,
         )
-    pl.semaphore_wait(barrier, len(peers))
     part = part[:ROWS] + part[ROWS:]
     part = part + pltpu.roll(part, RANK, 1)
     low_lanes = lax.broadcasted_iota(jnp.int32, (ROWS // 2, 2 * RANK), 1) < RANK
     lbuf[c * NX + x] = jnp.where(low_lanes, part[: ROWS // 2], part[ROWS // 2 :])
 
+    pl.semaphore_wait(barrier, len(peers))
     slot = lbuf.at[c * NX + x]
     lefts = send_all([(slot, slot, device(dx, 0, 0, dc)) for dx, dc in PLANEORDER], left_sem, 0, lbuf.at[0:7])
     away = merged.at[:, pl.ds(hint((1 - c) * HALF, 128), HALF)]
@@ -342,21 +342,14 @@
             update(cols)
 
     early = count // 2
-    first = [stage0(0)]
     gram = gram_start()
-    first += [stage0(n) for n in range(1, count)]
+    first = [stage0(n) for n in range(count)]
     gram = gram_middle(gram)
-    second = [stage1(n) for n in range(early)]
+    second = [stage1(n) for n in range(count)]
     gram = gram_end(gram)
-    second += [stage1(n) for n in range(early, count)]
-    third = [stage2(n) for n in range(early)]
+    third = [stage2(n) for n in range(count)]
     gram.wait_recv()
-    blocks = eliminate(gram_blocks(), 0, 16)
-    for n in range(early, count):
-        third.append(stage2(n))
-        if n < count - 1:
-            blocks = eliminate(blocks, 16, 32)
-    coefficients(eliminate(blocks, 32, RANK))
+    coefficients(eliminate(gram_blocks(), 0, RANK))
     for copy in late:
         copy.wait()
     fourth = []

time: 40.7 us -> 39.2 us (0.963)
  Pallas kernels: 40 us -> 38.5 us
    pallas_call x1, Pallas kernels: 37.6 us -> 36.1 us  [per_device(): pl.pallas_call(step_kernel, out_shape=shapes, in_specs=[hbm] * 6, out_spe...]
where the time goes in v5:
time: 39.2 us
  Pallas kernels  38.5 us (98%)
  between operations  0.64 us (2%)
    pallas_call x1, Pallas kernels, per_device(): pl.pallas_call(step_kernel, out_shape=shapes, in_specs=[hbm] * 6, out_spe...  36.1 us
    pallas_call x1, Pallas kernels, per_device(): pl.pallas_call(store_kernel, out_shape=shapes, in_specs=[vmem] * 5, out_s...  2.4 us

profile of v5, /device:TPU:1, one launch (start us, length us, event | category | flops | bytes accessed | tf_op | source)
XLA Modules:
  0.0 39.2 jit_solution(9394486621217504153)
XLA Ops:
  0.6 36.1 %shard_map.101 = (f32[48,5120]{1,0:T(8,128)S(1)}, f32[48,5120]{1,0:T(8,128)S(1)}, f32[48,5120]{1,0:T(8,128)S(1)}, f32[48,5120]{1,0:T(8,128)S(1)}, f32[64,5120]{1,0:T(8,128)S(1)}) custom-call(f32[48,5120]{1,0:T(8,128)} %bitcast.6, f32[48,5120]{1,0:T(8,128)} %bitcast.7, f32[64,5120]{1,0:T(8,128)} %bitcast.5, f32[48,5120]{1,0:T(8,128)} %weights.1, ...), custom_call_target="tpu_custom_call" | custom-call | tf_op jit(solution)/shard_map/pallas_call | solution.py:384
  36.8 2.4 %shard_map.102 = (f32[48,5120]{1,0:T(8,128)}, f32[48,5120]{1,0:T(8,128)}, f32[48,5120]{1,0:T(8,128)}, f32[48,5120]{1,0:T(8,128)}, f32[64,5120]{1,0:T(8,128)}) custom-call(f32[48,5120]{1,0:T(8,128)S(1)} %get-tuple-element.15.refs_0_, f32[48,5120]{1,0:T(8,128)S(1)} %get-tuple-element.16.refs_1_, f32[48,5120]{1,0:T(8,128)S(1)} %get-tuple-element.17.refs_2_, ...), custom_call_target="tpu_custom_call" | custom-call | tf_op jit(solution)/shard_map/pallas_call | solution.py:424

commit v6 on v5

--- a/solution.py
+++ b/solution.py
@@ -21,7 +21,7 @@
 HALF = D // 2
 PLANE = 896
 ZFIRST = HALF - 2 * PLANE
-CHUNKS = ((True, 0, 256), (False, 0, 384), (True, 256, 256), (False, 384, 256), (True, 512, 256), (False, 640, 256))
+CHUNKS = ((True, 0, 256), (False, 0, 256), (True, 256, 256), (False, 256, 256), (True, 512, 256), (False, 512, 256), (False, 768, 128))
 LOAD = 1280
 GROUP = 4
 ZORDER = (4, 3, 5, 2, 6, 1, 7)

time: 39.2 us -> 39 us (level)
  no operation moved by 1% of the time
where the time goes in v6:
time: 39 us; the launch traced here: 38.9 us
  Pallas kernels  38.3 us (98%)
  between operations  0.64 us (2%)
    pallas_call x1, Pallas kernels, per_device(): pl.pallas_call(step_kernel, out_shape=shapes, in_specs=[hbm] * 6, out_spe...  35.9 us
    pallas_call x1, Pallas kernels, per_device(): pl.pallas_call(store_kernel, out_shape=shapes, in_specs=[vmem] * 5, out_s...  2.4 us

profile of v6, /device:TPU:1, one launch (start us, length us, event | category | flops | bytes accessed | tf_op | source)
XLA Modules:
  0.0 38.9 jit_solution(14542158411786818832)
XLA Ops:
  0.6 35.9 %shard_map.101 = (f32[48,5120]{1,0:T(8,128)S(1)}, f32[48,5120]{1,0:T(8,128)S(1)}, f32[48,5120]{1,0:T(8,128)S(1)}, f32[48,5120]{1,0:T(8,128)S(1)}, f32[64,5120]{1,0:T(8,128)S(1)}) custom-call(f32[48,5120]{1,0:T(8,128)} %bitcast.6, f32[48,5120]{1,0:T(8,128)} %bitcast.7, f32[64,5120]{1,0:T(8,128)} %bitcast.5, f32[48,5120]{1,0:T(8,128)} %weights.1, ...), custom_call_target="tpu_custom_call" | custom-call | tf_op jit(solution)/shard_map/pallas_call | solution.py:384
  36.5 2.4 %shard_map.102 = (f32[48,5120]{1,0:T(8,128)}, f32[48,5120]{1,0:T(8,128)}, f32[48,5120]{1,0:T(8,128)}, f32[48,5120]{1,0:T(8,128)}, f32[64,5120]{1,0:T(8,128)}) custom-call(f32[48,5120]{1,0:T(8,128)S(1)} %get-tuple-element.15.refs_0_, f32[48,5120]{1,0:T(8,128)S(1)} %get-tuple-element.16.refs_1_, f32[48,5120]{1,0:T(8,128)S(1)} %get-tuple-element.17.refs_2_, ...), custom_call_target="tpu_custom_call" | custom-call | tf_op jit(solution)/shard_map/pallas_call | solution.py:424

commit v7 on v6

--- a/solution.py
+++ b/solution.py
@@ -342,8 +342,9 @@
             update(cols)
 
     early = count // 2
+    first = [stage0(0)]
     gram = gram_start()
-    first = [stage0(n) for n in range(count)]
+    first += [stage0(n) for n in range(1, count)]
     gram = gram_middle(gram)
     second = [stage1(n) for n in range(count)]
     gram = gram_end(gram)

time: 39 us -> 39 us (level)
  no operation moved by 1% of the time
where the time goes in v7:
time: 39 us; the launch traced here: 38.9 us
  Pallas kernels  38.2 us (98%)
  between operations  0.64 us (2%)
    pallas_call x1, Pallas kernels, per_device(): pl.pallas_call(step_kernel, out_shape=shapes, in_specs=[hbm] * 6, out_spe...  35.8 us
    pallas_call x1, Pallas kernels, per_device(): pl.pallas_call(store_kernel, out_shape=shapes, in_specs=[vmem] * 5, out_s...  2.4 us

profile of v7, /device:TPU:1, one launch (start us, length us, event | category | flops | bytes accessed | tf_op | source)
XLA Modules:
  0.0 38.9 jit_solution(2977974315639677562)
XLA Ops:
  0.6 35.8 %shard_map.101 = (f32[48,5120]{1,0:T(8,128)S(1)}, f32[48,5120]{1,0:T(8,128)S(1)}, f32[48,5120]{1,0:T(8,128)S(1)}, f32[48,5120]{1,0:T(8,128)S(1)}, f32[64,5120]{1,0:T(8,128)S(1)}) custom-call(f32[48,5120]{1,0:T(8,128)} %bitcast.6, f32[48,5120]{1,0:T(8,128)} %bitcast.7, f32[64,5120]{1,0:T(8,128)} %bitcast.5, f32[48,5120]{1,0:T(8,128)} %weights.1, ...), custom_call_target="tpu_custom_call" | custom-call | tf_op jit(solution)/shard_map/pallas_call | solution.py:385
  36.5 2.4 %shard_map.102 = (f32[48,5120]{1,0:T(8,128)}, f32[48,5120]{1,0:T(8,128)}, f32[48,5120]{1,0:T(8,128)}, f32[48,5120]{1,0:T(8,128)}, f32[64,5120]{1,0:T(8,128)}) custom-call(f32[48,5120]{1,0:T(8,128)S(1)} %get-tuple-element.15.refs_0_, f32[48,5120]{1,0:T(8,128)S(1)} %get-tuple-element.16.refs_1_, f32[48,5120]{1,0:T(8,128)S(1)} %get-tuple-element.17.refs_2_, ...), custom_call_target="tpu_custom_call" | custom-call | tf_op jit(solution)/shard_map/pallas_call | solution.py:425
